TPU v7x, 32 devices: a whole 2x2x4 slice. The times are simulated.
32 devices in a mesh: phi: 8 (over y, x, core), band: 4 (over z).
Axes of the slice: x: 2, y: 2, z: 4, core: 2. Of those that a mesh axis runs over, the one named last changes fastest.
Arguments:
- density: float32 [128, 64, 256], P('phi', 'band'), may hold values from 0.5 to 2
- velocity: float32 [3, 128, 64, 256], P(None, 'phi', 'band'), may hold values from -3 to 3
- magnetic_vector: float32 [3, 128, 64, 256], P(None, 'phi', 'band'), may hold values from -3 to 3
- pressure: float32 [128, 64, 256], P('phi', 'band'), may hold values from 0.2 to 2
- fluid_courant_number: float32 [], replicated, may hold values from 0.3 to 0.6
- cosmic_ray_density: float32 [64, 128, 64, 128], P('band', 'phi'), may hold values from 0.3 to 3
- diffusion_per_bin: float32 [64], replicated, may hold values from 0.15 to 0.5
- super_step_scale: float32 [], replicated, may hold values from 2 to 4
Outputs:
- fluid_state: float32 [8, 128, 64, 256], P(None, 'phi', 'band')
- cosmic_ray_next: float32 [64, 128, 64, 128], P('band', 'phi')
All inputs are finite; a program needn't handle non-finite values.
Results may differ from a plain program's by a relative error of at most 0.00125.
Values may be sent and summed in bfloat16 or wider, within the bound.
A program may use at most 256 MiB of HBM per device.

v0:
```python
import functools
import math

import jax
import jax.numpy as jnp
import numpy as np
from jax import lax
from jax.experimental import pallas as pl
from jax.experimental.pallas import tpu as pltpu
from jax.sharding import PartitionSpec as P

ADIABATIC = 5.0 / 3.0
INNER_RADIUS = 0.1
R_RATIO = 30.0
COLAT_LOW = math.pi / 6.0
COLAT_SPAN = 2.0 * math.pi / 3.0
P_RATIO = 1000.0
K_RATIO = 0.1
B_FLOOR = 0.1
V_BOUND = 3.0
B_BOUND = 3.0
P_HIGH = 2.0
RHO_LOW = 0.5
KAPPA_HIGH = 0.5


def grid_steps(n_radial, n_colat, n_azim, n_bins):
    return (
        math.log(R_RATIO) / n_radial,
        COLAT_SPAN / n_colat,
        2.0 * math.pi / n_azim,
        math.log(P_RATIO) / n_bins,
    )


def rate_limits(n_radial, n_shells, n_colat, n_azim, n_bins):
    radial_spacing, colatitude_spacing, azimuth_spacing, step_m = grid_steps(
        n_radial, n_colat, n_azim, n_bins
    )
    sine_lower = math.sin(COLAT_LOW + 0.5 * colatitude_spacing)
    fluid_radius = INNER_RADIUS * math.exp(0.5 * radial_spacing)
    fastest_limit = V_BOUND + math.sqrt((ADIABATIC * P_HIGH + 3.0 * B_BOUND**2) / RHO_LOW)
    fluid_rate = fastest_limit * (
        1.0 / (fluid_radius * radial_spacing)
        + 1.0 / (fluid_radius * colatitude_spacing)
        + 1.0 / (fluid_radius * sine_lower * azimuth_spacing)
    )
    shell_low = INNER_RADIUS * math.exp(radial_spacing * (n_radial - n_shells + 0.5))
    inv_r = 1.0 / (shell_low * radial_spacing)
    inv_t = 1.0 / (shell_low * colatitude_spacing)
    inv_p = 1.0 / (shell_low * sine_lower * azimuth_spacing)
    cosmic_ray_rate = (
        2.0 * KAPPA_HIGH * (inv_r**2 + inv_t**2 + inv_p**2)
        + V_BOUND * (inv_r + inv_t + inv_p)
        + V_BOUND * (inv_r + inv_t + inv_p + 4.0 / shell_low) / (3.0 * step_m)
    )
    return (fluid_rate, cosmic_ray_rate)


def fluid_cells(prim, normal):
    rho, v, b, pres = prim[0], prim[1:4], prim[4:7], prim[7]
    v_n, b_n = v[normal], b[normal]
    b_sq = b[0] * b[0] + b[1] * b[1] + b[2] * b[2]
    v_sq = v[0] * v[0] + v[1] * v[1] + v[2] * v[2]
    energy = pres * (1.0 / (ADIABATIC - 1.0)) + 0.5 * rho * v_sq + 0.5 * b_sq
    total_p = pres + 0.5 * b_sq
    mom = [rho * v[k] for k in range(3)]
    state = [rho] + mom + list(b) + [energy]
    push = [mom[k] * v_n - b[k] * b_n for k in range(3)]
    push[normal] = push[normal] + total_p
    turn = [v_n * b[k] - b_n * v[k] for k in range(3)]
    work = (energy + total_p) * v_n - b_n * (v[0] * b[0] + v[1] * b[1] + v[2] * b[2])
    speed = jnp.abs(v_n) + jnp.sqrt((ADIABATIC * pres + b_sq) / rho)
    return state, [mom[normal]] + push + turn + [work], speed


def face_flux(low, high):
    wave = jnp.maximum(low[2], high[2])
    return [
        0.5 * ((low[1][n] + high[1][n]) - wave * (high[0][n] - low[0][n])) for n in range(8)
    ]


MESH = pl.DeviceIdType.MESH
PAD = 8


def cosmic_ray_kernel(
    bands,
    phis,
    spacing,
    kappa_ref,
    tau_ref,
    dt_ref,
    rho_ref,
    vel_ref,
    mag_ref,
    pres_ref,
    inv_r_ref,
    inv_sin_ref,
    cot_ref,
    f_hbm,
    out_hbm,
    fluid_hbm,
    cells,
    firsts,
    coefs,
    wind,
    edge_t,
    edge_p,
    send_phi,
    send_bin,
    recv_phi,
    recv_bin,
    prims,
    fluid,
    edge_f,
    send_f,
    recv_f,
    fluid_sem,
    fluid_send,
    fluid_recv,
    load_sem,
    store_sem,
    wind_send,
    wind_recv,
    edge_t_send,
    edge_t_recv,
    edge_p_send,
    edge_p_recv,
    halo_send,
    halo_recv,
    next_send,
    next_recv,
):
    bins = f_hbm.shape[0]
    azim = f_hbm.shape[1]
    colat = f_hbm.shape[2]
    shells = f_hbm.shape[3]
    rows = colat // bands
    first_shell = vel_ref.shape[3] - shells
    step_r, step_t, step_p, step_m = spacing
    band = lax.axis_index("band")
    phi = lax.axis_index("phi")
    right = lax.rem(phi + 1, phis)
    left = lax.rem(phi + phis - 1, phis)

    load = pltpu.make_async_copy(
        f_hbm, cells.at[1 : bins + 1, 1 : azim + 1, PAD : PAD + colat], load_sem
    )
    load.start()

    barrier = pltpu.get_barrier_semaphore()
    for b in range(bands):
        for side in (left, right):
            pl.semaphore_signal(
                barrier, inc=1, device_id={"phi": side, "band": b}, device_id_type=MESH
            )
    for s in range(1, bands):
        pl.semaphore_signal(
            barrier,
            inc=1,
            device_id={"band": lax.rem(band + s, bands)},
            device_id_type=MESH,
        )

    own_rows = pl.ds(PAD, rows)

    def take(p, _):
        v = [vel_ref[c, p] for c in range(3)]
        b = [mag_ref[c, p] for c in range(3)]
        prim = [rho_ref[p]] + v + b + [pres_ref[p]]
        shell = [x[:, first_shell:].astype(jnp.bfloat16) for x in v + b]
        for c in range(6):
            wind[band, c, p] = shell[c]
        for n in range(8):
            prims[n, p + 1, own_rows] = prim[n]
            edge_f[0, n, p] = prim[n][rows - 1 : rows]
            edge_f[1, n, p] = prim[n][0:1]
        u_t = shell[1].astype(jnp.float32)
        edge_t[band, 0, pl.ds(p, 1), :] = u_t[0:1]
        edge_t[band, 1, pl.ds(p, 1), :] = u_t[rows - 1 : rows]
        return 0

    lax.fori_loop(0, azim, take, 0)
    edge_p[2, band] = wind[band, 2, azim - 1].astype(jnp.float32)
    edge_p[3, band] = wind[band, 2, 0].astype(jnp.float32)
    for n in range(8):
        send_f[0, n] = prims[n, azim, own_rows].astype(jnp.bfloat16)
        send_f[1, n] = prims[n, 1, own_rows].astype(jnp.bfloat16)
        for way in range(2):
            send_f[2 + way, n] = edge_f[way, n].reshape(azim, -1).astype(jnp.bfloat16)
    pl.semaphore_wait(barrier, 3 * bands - 1)

    def fluid_copy(way):
        if way < 2:
            target = {"phi": right if way == 0 else left}
        else:
            target = {"band": band + (1 if way == 2 else -1)}
        return pltpu.make_async_remote_copy(
            src_ref=send_f.at[way],
            dst_ref=recv_f.at[way],
            send_sem=fluid_send.at[way],
            recv_sem=fluid_recv.at[way],
            device_id=target,
            device_id_type=MESH,
        )

    def has(way):
        return band < bands - 1 if way == 0 else band > 0

    def comes(way):
        return band > 0 if way == 0 else band < bands - 1

    def wind_copy(way, s, block):
        return pltpu.make_async_remote_copy(
            src_ref=wind.at[block],
            dst_ref=wind.at[block],
            send_sem=wind_send.at[way, s],
            recv_sem=wind_recv.at[way, s],
            device_id={"band": band + (1 if way == 0 else -1)},
            device_id_type=MESH,
        )

    def edge_t_copy(s):
        return pltpu.make_async_remote_copy(
            src_ref=edge_t.at[band],
            dst_ref=edge_t.at[band],
            send_sem=edge_t_send.at[s - 1],
            recv_sem=edge_t_recv.at[s - 1],
            device_id={"band": lax.rem(band + s, bands)},
            device_id_type=MESH,
        )

    def edge_p_copy(way, b):
        return pltpu.make_async_remote_copy(
            src_ref=edge_p.at[2 + way, band],
            dst_ref=edge_p.at[way, band],
            send_sem=edge_p_send.at[way, b],
            recv_sem=edge_p_recv.at[way, band],
            device_id={"phi": right if way == 0 else left, "band": b},
            device_id_type=MESH,
        )

    @pl.when(band < bands - 1)
    def _():
        wind_copy(0, 0, band).start()

    @pl.when(band > 0)
    def _():
        wind_copy(1, 0, band).start()

    for way in range(2):

        @pl.when(has(way))
        def _(way=way):
            fluid_copy(2 + way).start()

        fluid_copy(way).start()
    for s in range(1, bands):
        edge_t_copy(s).start()
    for b in range(bands):
        for way in range(2):
            edge_p_copy(way, b).start()

    def phi_copy(stage, way, block):
        part = pl.ds(pl.multiple_of(block * rows, rows), rows)
        sems = (next_send, next_recv)
        return pltpu.make_async_remote_copy(
            src_ref=send_phi.at[stage, way, :, part],
            dst_ref=recv_phi.at[stage, way, :, part],
            send_sem=sems[0].at[way, block],
            recv_sem=sems[1].at[way, block],
            device_id={"phi": right if way == 0 else left},
            device_id_type=MESH,
        )

    def bin_copy(stage, way, block):
        part = pl.ds(pl.multiple_of(block * rows, rows), rows)
        return pltpu.make_async_remote_copy(
            src_ref=send_bin.at[stage, way, :, part],
            dst_ref=recv_bin.at[stage, way, :, part],
            send_sem=next_send.at[2 + way, block],
            recv_sem=next_recv.at[2 + way, block],
            device_id={"band": band + (1 if way == 0 else -1)},
            device_id_type=MESH,
        )

    def whole_phi(way):
        return pltpu.make_async_remote_copy(
            src_ref=send_phi.at[0, way],
            dst_ref=recv_phi.at[0, way],
            send_sem=halo_send.at[way],
            recv_sem=halo_recv.at[way],
            device_id={"phi": right if way == 0 else left},
            device_id_type=MESH,
        )

    def whole_bin(way):
        return pltpu.make_async_remote_copy(
            src_ref=send_bin.at[0, way],
            dst_ref=recv_bin.at[0, way],
            send_sem=halo_send.at[2 + way],
            recv_sem=halo_recv.at[2 + way],
            device_id={"band": band + (1 if way == 0 else -1)},
            device_id_type=MESH,
        )

    def stage_out(stage, source, start, count):
        own = pl.ds(start, count)
        inner = pl.ds(PAD + start, count)

        def phi_part(k, _):
            last, lead = source[k + 1, azim, inner], source[k + 1, 1, inner]
            send_phi[stage, 0, k, own] = last.astype(jnp.bfloat16)
            send_phi[stage, 1, k, own] = lead.astype(jnp.bfloat16)
            return 0

        def bin_part(p, _):
            last, lead = source[bins, p + 1, inner], source[1, p + 1, inner]
            send_bin[stage, 0, p, own] = last.astype(jnp.bfloat16)
            send_bin[stage, 1, p, own] = lead.astype(jnp.bfloat16)
            return 0

        lax.fori_loop(0, bins, phi_part, 0)
        lax.fori_loop(0, azim, bin_part, 0)

    def stage_in_phi(stage, target, start, count):
        own = pl.ds(start, count)
        inner = pl.ds(PAD + start, count)

        def phi_part(k, _):
            target[k + 1, 0, inner] = recv_phi[stage, 0, k, own].astype(jnp.float32)
            target[k + 1, azim + 1, inner] = recv_phi[stage, 1, k, own].astype(jnp.float32)
            return 0

        lax.fori_loop(0, bins, phi_part, 0)

    def stage_in_bin(stage, target):
        inner = pl.ds(PAD, colat)
        for way, ghost, edge in ((0, 0, 1), (1, bins + 1, bins)):

            @pl.when(comes(way))
            def _(way=way, ghost=ghost):
                def bin_part(p, _):
                    target[ghost, p + 1, inner] = recv_bin[stage, way, p].astype(jnp.float32)
                    return 0

                lax.fori_loop(0, azim, bin_part, 0)

            @pl.when(jnp.logical_not(comes(way)))
            def _(ghost=ghost, edge=edge):
                def bin_part(p, _):
                    target[ghost, p + 1, inner] = target[edge, p + 1, inner]
                    return 0

                lax.fori_loop(0, azim, bin_part, 0)

    def pad_colat(target):
        def part(p, _):
            low = [target[k + 1, p + 1, PAD : PAD + 1] for k in range(bins)]
            high = [target[k + 1, p + 1, PAD + colat - 1 : PAD + colat] for k in range(bins)]
            for k in range(bins):
                target[k + 1, p + 1, PAD - 1 : PAD] = low[k]
                target[k + 1, p + 1, PAD + colat : PAD + colat + 1] = high[k]
            return 0

        lax.fori_loop(0, azim, part, 0)

    load.wait()
    stage_out(0, cells, 0, colat)
    for way in range(2):

        @pl.when(has(way))
        def _(way=way):
            whole_bin(way).start()

        whole_phi(way).start()
    pad_colat(cells)

    lane = lax.broadcasted_iota(jnp.int32, (rows, shells), 1)
    row = lax.broadcasted_iota(jnp.int32, (rows, shells), 0)
    tau = tau_ref[0]
    inv_r = jnp.broadcast_to(inv_r_ref[0:1, first_shell:], (rows, shells))
    inv_hr = inv_r * (1.0 / step_r)
    inv_ht = inv_r * (1.0 / step_t)

    def make_coefs(block):
        start = pl.multiple_of(block * rows, rows)
        part = pl.ds(start, rows)
        inv_hp = inv_r * inv_sin_ref[part, :shells] * (1.0 / step_p)
        cot_r = inv_r * cot_ref[part, :shells]
        below = jnp.maximum(block - 1, 0)
        above = jnp.minimum(block + 1, bands - 1)

        def one(p):
            u_r, u_t, u_p, b_r, b_t, b_p = [
                wind[block, c, p].astype(jnp.float32) for c in range(6)
            ]
            r_hi = jnp.where(lane == shells - 1, u_r, pltpu.roll(u_r, shells - 1, 1))
            r_lo = jnp.where(lane == 0, u_r, pltpu.roll(u_r, 1, 1))
            t_hi_row = jnp.where(
                block == bands - 1, u_t[rows - 1 : rows], edge_t[above, 0, pl.ds(p, 1), :]
            )
            t_lo_row = jnp.where(block == 0, u_t[0:1], edge_t[below, 1, pl.ds(p, 1), :])
            t_hi = jnp.where(row == rows - 1, t_hi_row, pltpu.roll(u_t, rows - 1, 0))
            t_lo = jnp.where(row == 0, t_lo_row, pltpu.roll(u_t, 1, 0))
            p_hi = jnp.where(
                p == azim - 1,
                edge_p[1, block],
                wind[block, 2, jnp.minimum(p + 1, azim - 1)].astype(jnp.float32),
            )
            p_lo = jnp.where(
                p == 0,
                edge_p[0, block],
                wind[block, 2, jnp.maximum(p - 1, 0)].astype(jnp.float32),
            )
            spread = (
                (r_hi - r_lo) * (0.5 * inv_hr)
                + 2.0 * u_r * inv_r
                + (t_hi - t_lo) * (0.5 * inv_ht)
                + cot_r * u_t
                + (p_hi - p_lo) * (0.5 * inv_hp)
            )
            spread = spread.astype(jnp.bfloat16).astype(jnp.float32)
            share = (1.0 - K_RATIO) / (b_r * b_r + b_t * b_t + b_p * b_p + B_FLOOR)
            c_r = tau * (K_RATIO + share * b_r * b_r) * inv_hr * inv_hr
            c_t = tau * (K_RATIO + share * b_t * b_t) * inv_ht * inv_ht
            c_p = tau * (K_RATIO + share * b_p * b_p) * inv_hp * inv_hp
            c_rp = jnp.where(lane == shells - 1, 0.0, c_r)
            c_rm = jnp.where(lane == 0, 0.0, c_r)
            a_r = tau * u_r * inv_hr
            a_r = jnp.where((lane == 0) & (a_r > 0.0), 0.0, a_r)
            a_r = jnp.where((lane == shells - 1) & (a_r < 0.0), 0.0, a_r)
            a_t = tau * u_t * inv_ht
            a_p = tau * u_p * inv_hp
            mu = tau * spread * (1.0 / (3.0 * step_m))
            c_sum = c_rp + c_rm + 2.0 * c_t + 2.0 * c_p
            a_sum = 1.0 - (jnp.abs(a_r) + jnp.abs(a_t) + jnp.abs(a_p) + jnp.abs(mu))
            return (c_rp, c_rm, c_t, c_p, a_r, a_t, a_p, mu, c_sum, a_sum)

        def pair(i, _):
            both = [one(2 * i), one(2 * i + 1)]
            for j in range(2):
                for n, value in enumerate(both[j]):
                    coefs[n, 2 * i + j, part] = value
            return 0

        lax.fori_loop(0, azim // 2, pair, 0)

    def apply(source, p, start, finish, low_bin, high_bin):
        part = pl.ds(start, 8)
        mid = pl.ds(PAD + start, 8)
        low = pl.ds(PAD + start - 1, 8)
        high = pl.ds(PAD + start + 1, 8)
        c_rp, c_rm, c_t, c_p, a_r, a_t, a_p, mu, c_sum, a_sum = [
            coefs[n, p, part] for n in range(10)
        ]
        w_r, w_t, w_p, w_m = jnp.abs(a_r), jnp.abs(a_t), jnp.abs(a_p), jnp.abs(mu)
        out_r, out_t, out_p, up_m = a_r > 0.0, a_t > 0.0, a_p > 0.0, mu > 0.0
        values = []
        before = source[low_bin, p + 1, mid]
        here = source[low_bin + 1, p + 1, mid]
        for k in range(low_bin, high_bin):
            after = source[k + 2, p + 1, mid]
            kappa = kappa_ref[band * bins + k]
            r_hi = pltpu.roll(here, shells - 1, 1)
            r_lo = pltpu.roll(here, 1, 1)
            t_hi = source[k + 1, p + 1, high]
            t_lo = source[k + 1, p + 1, low]
            p_hi = source[k + 1, p + 2, mid]
            p_lo = source[k + 1, p, mid]
            curve = (
                (c_rp * r_hi + c_rm * r_lo)
                + (c_t * (t_hi + t_lo) + c_p * (p_hi + p_lo))
                - c_sum * here
            )
            flow = (
                (w_r * jnp.where(out_r, r_lo, r_hi) + w_t * jnp.where(out_t, t_lo, t_hi))
                + (w_p * jnp.where(out_p, p_lo, p_hi) + w_m * jnp.where(up_m, after, before))
                + a_sum * here
            )
            values.append(finish(k, p, mid, kappa * curve + flow))
            before, here = here, after
        return [
            (k + 1, mid, value) for k, value in zip(range(low_bin, high_bin), values)
        ]

    def keep(target, p, results):
        for k, mid, value in results:
            target[k, p + 1, mid] = value

    def finish_first(k, p, mid, value):
        return value

    def finish_second(k, p, mid, value):
        return 1.5 * value - 0.5 * cells[k + 1, p + 1, mid]

    def fluid_in():
        for n in range(8):
            prims[n, 0, own_rows] = recv_f[0, n].astype(jnp.float32)
            prims[n, azim + 1, own_rows] = recv_f[1, n].astype(jnp.float32)
        for way, ghost, edge in ((0, PAD - 1, PAD), (1, PAD + rows, PAD + rows - 1)):
            at = pl.ds(ghost, 1)

            @pl.when(comes(way))
            def _(way=way, at=at):
                for n in range(8):
                    edge_f[way, n] = recv_f[2 + way, n].astype(jnp.float32).reshape(azim, 1, -1)

                def part(p, _):
                    for n in range(8):
                        prims[n, p + 1, at] = edge_f[way, n, p]
                    return 0

                lax.fori_loop(0, azim, part, 0)

            @pl.when(jnp.logical_not(comes(way)))
            def _(at=at, edge=edge):
                def part(p, _):
                    for n in range(8):
                        prims[n, p + 1, at] = prims[n, p + 1, pl.ds(edge, 1)]
                    return 0

                lax.fori_loop(0, azim, part, 0)

    def fluid_step():
        radial = vel_ref.shape[3]
        spot = lax.broadcasted_iota(jnp.int32, (8, radial), 1)
        scale = dt_ref[0] * inv_r_ref[0:8, :]

        for start in range(0, rows, 8):
            here_rows = pl.ds(pl.multiple_of(band * rows + start, 8), 8)
            scale_p = (1.0 / step_p) * scale * inv_sin_ref[here_rows, :]

            def load_cells(p, shift, start=start):
                return [prims[n, p, pl.ds(PAD + start + shift, 8)] for n in range(8)]

            def faces(p, lower, start=start, scale_p=scale_p, load_cells=load_cells):
                mine = load_cells(p + 1, 0)
                upper = face_flux(
                    fluid_cells(mine, 2), fluid_cells(load_cells(p + 2, 0), 2)
                )
                total = [scale_p * (upper[n] - lower[n]) for n in range(8)]
                here = fluid_cells(mine, 1)
                low = face_flux(fluid_cells(load_cells(p + 1, -1), 1), here)
                high = face_flux(here, fluid_cells(load_cells(p + 1, 1), 1))
                scale_t = (1.0 / step_t) * scale
                total = [total[n] + scale_t * (high[n] - low[n]) for n in range(8)]
                state, flux, speed = fluid_cells(mine, 0)

                def ahead(value):
                    return jnp.where(spot == radial - 1, value, pltpu.roll(value, radial - 1, 1))

                outer = face_flux(
                    (state, flux, speed),
                    ([ahead(x) for x in state], [ahead(x) for x in flux], ahead(speed)),
                )
                scale_r = (1.0 / step_r) * scale
                for n in range(8):
                    inner = jnp.where(spot == 0, flux[n], pltpu.roll(outer[n], 1, 1))
                    fluid[n, p, pl.ds(start, 8)] = state[n] - (
                        total[n] + scale_r * (outer[n] - inner)
                    )
                return upper

            first = face_flux(
                fluid_cells(load_cells(0, 0), 2), fluid_cells(load_cells(1, 0), 2)
            )
            lax.fori_loop(0, azim, faces, first)

    for way in range(2):

        @pl.when(has(way))
        def _(way=way):
            fluid_copy(2 + way).wait_send()

        @pl.when(comes(way))
        def _(way=way):
            fluid_copy(2 + way).wait_recv()

        fluid_copy(way).wait()
    fluid_in()
    fluid_step()
    fluid_store = pltpu.make_async_copy(fluid, fluid_hbm, fluid_sem)
    fluid_store.start()
    for s in range(1, bands):
        edge_t_copy(s).wait()
    for b in range(bands):
        for way in range(2):
            edge_p_copy(way, b).wait_send()
            pltpu.make_async_remote_copy(
                src_ref=edge_p.at[2 + way, b],
                dst_ref=edge_p.at[way, b],
                send_sem=edge_p_send.at[way, b],
                recv_sem=edge_p_recv.at[way, b],
                device_id={"phi": right if way == 0 else left, "band": b},
                device_id_type=MESH,
            ).wait_recv()
    make_coefs(band)
    for way in range(2):

        @pl.when(has(way))
        def _(way=way):
            whole_bin(way).wait_send()

        @pl.when(comes(way))
        def _(way=way):
            whole_bin(way).wait_recv()

        whole_phi(way).wait()
    stage_in_phi(0, cells, 0, colat)
    stage_in_bin(0, cells)

    def second_inner(block):
        start = pl.multiple_of(block * rows, rows)
        for way in range(2):
            phi_copy(1, way, block).wait_recv()
        stage_in_phi(1, firsts, start, rows)

        @pl.when((block == 0) | (block == bands - 1))
        def _():
            pad = jnp.where(block == 0, PAD - 1, PAD + colat)
            edge = jnp.where(block == 0, PAD, PAD + colat - 1)

            def part(p, _):
                rim = [firsts[k + 1, p + 1, pl.ds(edge, 1)] for k in range(bins)]
                for k in range(bins):
                    firsts[k + 1, p + 1, pl.ds(pad, 1)] = rim[k]
                return 0

            lax.fori_loop(0, azim, part, 0)

        def one(p, _):
            results = []
            for part in range(rows // 8):
                results += apply(firsts, p, start + 8 * part, finish_second, 1, bins - 1)
            keep(cells, p, results)
            return 0

        lax.fori_loop(0, azim, one, 0)

    def visit(i, _):
        s = (i + 1) // 2
        below = lax.rem(i, 2) == 1
        block = jnp.where(below, band - s, band + s)
        valid = (block >= 0) & (block < bands)

        @pl.when(valid & below)
        def _():
            wind_copy(0, s - 1, block).wait_recv()

            @pl.when(band < bands - 1)
            def _():
                wind_copy(0, s, block).start()

        @pl.when(valid & jnp.logical_not(below) & (s > 0))
        def _():
            wind_copy(1, s - 1, block).wait_recv()

            @pl.when(band > 0)
            def _():
                wind_copy(1, s, block).start()

        @pl.when(valid)
        def _():
            @pl.when(s > 0)
            def _():
                make_coefs(block)

            start = pl.multiple_of(block * rows, rows)

            def one(p, _):
                results = []
                for part in range(rows // 8):
                    results += apply(cells, p, start + 8 * part, finish_first, 0, bins)
                keep(firsts, p, results)
                return 0

            lax.fori_loop(0, azim, one, 0)
            stage_out(1, firsts, start, rows)
            for way in range(2):

                @pl.when(has(way))
                def _(way=way):
                    bin_copy(1, way, block).start()

                phi_copy(1, way, block).start()

            inner = (s >= 2) | ((s == 1) & (jnp.logical_not(below) | (band == bands - 1)))
            outer = (s >= 1) & ((block == 0) | (block == bands - 1))

            def ready(t, _):
                @pl.when(jnp.where(t == 0, inner, outer))
                def _():
                    second_inner(jnp.where(t == 0, block + jnp.where(below, 1, -1), block))

                return 0

            lax.fori_loop(0, 2, ready, 0)

        return 0

    lax.fori_loop(0, 2 * bands - 1, visit, 0)
    for block in range(bands):
        for way in range(2):

            @pl.when(has(way))
            def _(way=way, block=block):
                bin_copy(1, way, block).wait_send()

            @pl.when(comes(way))
            def _(way=way, block=block):
                bin_copy(1, way, block).wait_recv()

            phi_copy(1, way, block).wait_send()
    stage_in_bin(1, firsts)

    def store(p):
        return pltpu.make_async_copy(
            cells.at[1 : bins + 1, p + 1, PAD : PAD + colat], out_hbm.at[:, p], store_sem.at[p]
        )

    group = math.gcd(colat // 8, 8)

    def second(p, _):
        def one(j, _):
            results = []
            for part in range(group):
                start = pl.multiple_of((j * group + part) * 8, 8)
                results += apply(firsts, p, start, finish_second, 0, 1)
                results += apply(firsts, p, start, finish_second, bins - 1, bins)
            keep(cells, p, results)
            return 0

        lax.fori_loop(0, colat // (8 * group), one, 0)
        store(p).start()
        return 0

    lax.fori_loop(0, azim, second, 0)

    def stored(p, _):
        store(p).wait()
        return 0

    lax.fori_loop(0, azim, stored, 0)
    fluid_store.wait()
    for s in range(bands - 1):

        @pl.when((band - s >= 0) & (band < bands - 1))
        def _(s=s):
            wind_copy(0, s, band - s).wait_send()

        @pl.when((band + s < bands) & (band > 0))
        def _(s=s):
            wind_copy(1, s, band + s).wait_send()


def deliver_kernel(ray_in, fluid_in, ray_out, fluid_out, ray, fluid, in_sem, out_sem):
    parts = [(fluid_in, fluid, fluid_out, n) for n in range(8)]
    parts += [(ray_in, ray, ray_out, k) for k in range(ray.shape[0])]
    loads = [
        pltpu.make_async_copy(a.at[n], b.at[n], in_sem.at[i])
        for i, (a, b, _, n) in enumerate(parts)
    ]
    stores = [
        pltpu.make_async_copy(b.at[n], c.at[n], out_sem.at[i])
        for i, (_, b, c, n) in enumerate(parts)
    ]
    for copy in loads:
        copy.start()
    for load, store in zip(loads, stores):
        load.wait()
        store.start()
    for copy in stores:
        copy.wait()


def cosmic_ray_step(
    rho, velocity, mag, pres, density, kappa, tau, dt, bands, phis, spacing
):
    bins, azim, colat, shells = density.shape
    radial = velocity.shape[3]
    rows = colat // bands
    radius = INNER_RADIUS * np.exp(
        math.log(R_RATIO) / radial * (np.arange(radial) + 0.5)
    )
    theta = COLAT_LOW + COLAT_SPAN * (np.arange(colat) + 0.5) / colat
    wide = np.ones((colat, radial))
    inv_r = jnp.asarray(np.broadcast_to(1.0 / radius, (8, radial)), jnp.float32)
    inv_sin = jnp.asarray(wide / np.sin(theta)[:, None], jnp.float32)
    cot = jnp.asarray(wide * (np.cos(theta) / np.sin(theta))[:, None], jnp.float32)
    dma = pltpu.SemaphoreType.DMA
    vmem = pl.BlockSpec(memory_space=pltpu.VMEM)
    smem = pl.BlockSpec(memory_space=pltpu.SMEM)
    hbm = pl.BlockSpec(memory_space=pl.ANY)
    padded_shape = (bins + 2, azim + 2, colat + 2 * PAD, shells)
    stepped, fluid = pl.pallas_call(
        functools.partial(cosmic_ray_kernel, bands, phis, spacing),
        out_shape=(
            jax.ShapeDtypeStruct(density.shape, jnp.float32),
            jax.ShapeDtypeStruct((8, azim, rows, radial), jnp.float32),
        ),
        in_specs=[smem, smem, smem, vmem, vmem, vmem, vmem, vmem, vmem, vmem, hbm],
        out_specs=(hbm, hbm),
        scratch_shapes=[
            pltpu.VMEM(padded_shape, jnp.float32),
            pltpu.VMEM(padded_shape, jnp.float32),
            pltpu.VMEM((10, azim, colat, shells), jnp.float32),
            pltpu.VMEM((bands, 6, azim, rows, shells), jnp.bfloat16),
            pltpu.VMEM((bands, 2, azim, shells), jnp.float32),
            pltpu.VMEM((4, bands, rows, shells), jnp.float32),
            pltpu.VMEM((2, 2, bins, colat, shells), jnp.bfloat16),
            pltpu.VMEM((2, 2, azim, colat, shells), jnp.bfloat16),
            pltpu.VMEM((2, 2, bins, colat, shells), jnp.bfloat16),
            pltpu.VMEM((2, 2, azim, colat, shells), jnp.bfloat16),
            pltpu.VMEM((8, azim + 2, rows + 2 * PAD, radial), jnp.float32),
            pltpu.VMEM((8, azim, rows, radial), jnp.float32),
            pltpu.VMEM((2, 8, azim, 1, radial), jnp.float32),
            pltpu.VMEM((4, 8, rows, radial), jnp.bfloat16),
            pltpu.VMEM((4, 8, rows, radial), jnp.bfloat16),
            dma,
            dma((4,)),
            dma((4,)),
            dma,
            dma((azim,)),
            dma((2, bands)),
            dma((2, bands)),
            dma((bands,)),
            dma((bands,)),
            dma((2, bands)),
            dma((2, bands)),
            dma((4,)),
            dma((4,)),
            dma((4, bands)),
            dma((4, bands)),
        ],
        compiler_params=pltpu.CompilerParams(
            collective_id=0, has_side_effects=True, vmem_limit_bytes=60 * 1024 * 1024
        ),
        cost_estimate=pl.CostEstimate(
            flops=80 * density.size, bytes_accessed=8 * density.size, transcendentals=0
        ),
        name="cosmic_ray",
    )(kappa, tau, dt, rho, velocity, mag, pres, inv_r, inv_sin, cot, density)
    return pl.pallas_call(
        deliver_kernel,
        out_shape=(
            jax.ShapeDtypeStruct(stepped.shape, jnp.float32),
            jax.ShapeDtypeStruct(fluid.shape, jnp.float32),
        ),
        in_specs=[hbm, hbm],
        out_specs=(hbm, hbm),
        scratch_shapes=[
            pltpu.VMEM(stepped.shape, jnp.float32),
            pltpu.VMEM(fluid.shape, jnp.float32),
            dma((bins + 8,)),
            dma((bins + 8,)),
        ],
        compiler_params=pltpu.CompilerParams(vmem_limit_bytes=60 * 1024 * 1024),
        name="deliver",
    )(stepped, fluid)


def body(
    density,
    velocity,
    magnetic_vector,
    pressure,
    fluid_courant_number,
    cosmic_ray_density,
    diffusion_per_bin,
    super_step_scale,
):
    azim_dev = density.shape[0]
    colat_dev = density.shape[1]
    radial_cell_count = density.shape[2]
    band_count = lax.axis_size("band")
    phi_count = lax.axis_size("phi")
    colatitude_count = colat_dev * band_count
    azimuth_cell_count = azim_dev * phi_count
    bin_dev = cosmic_ray_density.shape[0]
    momentum_bin_count = bin_dev * band_count
    outer_shell_count = cosmic_ray_density.shape[3]
    mesh_spacing = grid_steps(
        radial_cell_count, colatitude_count, azimuth_cell_count, momentum_bin_count
    )
    fluid_rate, cosmic_ray_rate = rate_limits(
        radial_cell_count,
        outer_shell_count,
        colatitude_count,
        azimuth_cell_count,
        momentum_bin_count,
    )
    cosmic_ray_next, fluid_state = cosmic_ray_step(
        density,
        velocity,
        magnetic_vector,
        pressure,
        cosmic_ray_density,
        diffusion_per_bin,
        (super_step_scale / (3.0 * cosmic_ray_rate)).reshape(1),
        (fluid_courant_number / fluid_rate).reshape(1),
        band_count,
        phi_count,
        mesh_spacing,
    )
    return (fluid_state, cosmic_ray_next)


def solution(mesh):
    placed = (
        P("phi", "band", None),
        P(None, "phi", "band", None),
        P(None, "phi", "band", None),
        P("phi", "band", None),
        P(),
        P("band", "phi", None, None),
        P(),
        P(),
    )
    return jax.shard_map(
        body,
        mesh=mesh,
        in_specs=placed,
        out_specs=(P(None, "phi", "band", None), P("band", "phi", None, None)),
        check_vma=False,
    )
```

profile of v0, /device:TPU:0, one launch (start us, length us, event | category | flops | bytes accessed | tf_op | source)
XLA Modules:
  0.0 86.2 jit_solution(3656993462314648071)
XLA Ops:
  1.9 76.2 %cosmic_ray.1 = (f32[16,16,64,128]{3,2,1,0:T(8,128)}, f32[8,16,16,256]{3,2,1,0:T(8,128)}) custom-call(f32[64]{0:T(128)} %kappa_ref.1, f32[1]{0:T(128)} %bitcast.tau_ref, f32[1]{0:T(128)} %bitcast.1.dt_ref, f32[16,16,256]{2,1,0:T(8,128)} %rho_ref.1, f32[3,16,16,256]{3,2,1,0:T(8,128)} %vel_ref.1, f32[3,16,16,256]{3,2,1,0:T(8,128)} %mag_ref.1, ...), custom_call_target="tpu_custom_call" | custom-call | flops 167772160 | bytes 16777216 | tf_op jit(solution)/shard_map/cosmic_ray/pallas_call | solution.py:798
  78.1 8.1 %deliver.1 = (f32[16,16,64,128]{3,2,1,0:T(8,128)}, f32[8,16,16,256]{3,2,1,0:T(8,128)}) custom-call(f32[16,16,64,128]{3,2,1,0:T(8,128)} %get-tuple-element.6.ray_in, f32[8,16,16,256]{3,2,1,0:T(8,128)} %get-tuple-element.7.fluid_in), custom_call_target="tpu_custom_call" | custom-call | tf_op jit(solution)/shard_map/deliver/pallas_call | solution.py:846
where the time goes:
time: 86.4 us; the launch traced here: 86.2 us
  Pallas kernels  84.3 us (98%)
  between operations  1.93 us (2%)
    pallas_call x1, Pallas kernels, cosmic_ray_step(): pl.pallas_call(functools.partial(cosmic_ray_kernel, bands, phis, spacing)...  76.2 us
    pallas_call x1, Pallas kernels, cosmic_ray_step(): pl.pallas_call(deliver_kernel, out_shape=(jax.ShapeDtypeStruct(stepped.sh...  8.1 us

commit v1 on v0

--- a/solution.py
+++ b/solution.py
@@ -322,8 +322,8 @@
             send_bin[stage, 1, p, own] = lead.astype(jnp.bfloat16)
             return 0
 
-        lax.fori_loop(0, bins, phi_part, 0)
-        lax.fori_loop(0, azim, bin_part, 0)
+        lax.fori_loop(0, bins, phi_part, 0, unroll=2)
+        lax.fori_loop(0, azim, bin_part, 0, unroll=2)
 
     def stage_in_phi(stage, target, start, count):
         own = pl.ds(start, count)
@@ -334,7 +334,7 @@
             target[k + 1, azim + 1, inner] = recv_phi[stage, 1, k, own].astype(jnp.float32)
             return 0
 
-        lax.fori_loop(0, bins, phi_part, 0)
+        lax.fori_loop(0, bins, phi_part, 0, unroll=2)
 
     def stage_in_bin(stage, target):
         inner = pl.ds(PAD, colat)
@@ -346,7 +346,7 @@
                     target[ghost, p + 1, inner] = recv_bin[stage, way, p].astype(jnp.float32)
                     return 0
 
-                lax.fori_loop(0, azim, bin_part, 0)
+                lax.fori_loop(0, azim, bin_part, 0, unroll=2)
 
             @pl.when(jnp.logical_not(comes(way)))
             def _(ghost=ghost, edge=edge):
@@ -354,7 +354,7 @@
                     target[ghost, p + 1, inner] = target[edge, p + 1, inner]
                     return 0
 
-                lax.fori_loop(0, azim, bin_part, 0)
+                lax.fori_loop(0, azim, bin_part, 0, unroll=2)
 
     def pad_colat(target):
         def part(p, _):
@@ -440,13 +440,13 @@
             return (c_rp, c_rm, c_t, c_p, a_r, a_t, a_p, mu, c_sum, a_sum)
 
         def pair(i, _):
-            both = [one(2 * i), one(2 * i + 1)]
-            for j in range(2):
-                for n, value in enumerate(both[j]):
-                    coefs[n, 2 * i + j, part] = value
+            several = [one(4 * i + j) for j in range(4)]
+            for j in range(4):
+                for n, value in enumerate(several[j]):
+                    coefs[n, 4 * i + j, part] = value
             return 0
 
-        lax.fori_loop(0, azim // 2, pair, 0)
+        lax.fori_loop(0, azim // 4, pair, 0)
 
     def apply(source, p, start, finish, low_bin, high_bin):
         part = pl.ds(start, 8)
@@ -509,8 +509,9 @@
                     edge_f[way, n] = recv_f[2 + way, n].astype(jnp.float32).reshape(azim, 1, -1)
 
                 def part(p, _):
+                    rim = [edge_f[way, n, p] for n in range(8)]
                     for n in range(8):
-                        prims[n, p + 1, at] = edge_f[way, n, p]
+                        prims[n, p + 1, at] = rim[n]
                     return 0
 
                 lax.fori_loop(0, azim, part, 0)
@@ -518,8 +519,9 @@
             @pl.when(jnp.logical_not(comes(way)))
             def _(at=at, edge=edge):
                 def part(p, _):
+                    rim = [prims[n, p + 1, pl.ds(edge, 1)] for n in range(8)]
                     for n in range(8):
-                        prims[n, p + 1, at] = prims[n, p + 1, pl.ds(edge, 1)]
+                        prims[n, p + 1, at] = rim[n]
                     return 0
 
                 lax.fori_loop(0, azim, part, 0)
@@ -631,14 +633,15 @@
 
             lax.fori_loop(0, azim, part, 0)
 
-        def one(p, _):
-            results = []
-            for part in range(rows // 8):
-                results += apply(firsts, p, start + 8 * part, finish_second, 1, bins - 1)
-            keep(cells, p, results)
+        def one(i, _):
+            for p in (2 * i, 2 * i + 1):
+                for part in range(rows // 8):
+                    keep(
+                        cells, p, apply(firsts, p, start + 8 * part, finish_second, 1, bins - 1)
+                    )
             return 0
 
-        lax.fori_loop(0, azim, one, 0)
+        lax.fori_loop(0, azim // 2, one, 0)
 
     def visit(i, _):
         s = (i + 1) // 2
@@ -670,14 +673,13 @@
 
             start = pl.multiple_of(block * rows, rows)
 
-            def one(p, _):
-                results = []
-                for part in range(rows // 8):
-                    results += apply(cells, p, start + 8 * part, finish_first, 0, bins)
-                keep(firsts, p, results)
+            def one(i, _):
+                for p in (2 * i, 2 * i + 1):
+                    for part in range(rows // 8):
+                        keep(firsts, p, apply(cells, p, start + 8 * part, finish_first, 0, bins))
                 return 0
 
-            lax.fori_loop(0, azim, one, 0)
+            lax.fori_loop(0, azim // 2, one, 0)
             stage_out(1, firsts, start, rows)
             for way in range(2):
 

time: 86.4 us -> 83.7 us (0.969)
  Pallas kernels: 84.3 us -> 81.6 us
    pallas_call x1, Pallas kernels: 76.2 us -> 73.5 us  [cosmic_ray_step(): pl.pallas_call(functools.partial(cosmic_ray_kernel, bands, phis, spacing)...]
where the time goes in v1:
time: 83.7 us; the launch traced here: 83.5 us
  Pallas kernels  81.6 us (97%)
  between operations  1.93 us (2%)
    pallas_call x1, Pallas kernels, cosmic_ray_step(): pl.pallas_call(functools.partial(cosmic_ray_kernel, bands, phis, spacing)...  73.5 us
    pallas_call x1, Pallas kernels, cosmic_ray_step(): pl.pallas_call(deliver_kernel, out_shape=(jax.ShapeDtypeStruct(stepped.sh...  8.1 us

profile of v1, /device:TPU:0, one launch (start us, length us, event | category | flops | bytes accessed | tf_op | source)
XLA Modules:
  0.0 83.5 jit_solution(13655762580690669360)
XLA Ops:
  1.9 73.5 %cosmic_ray.1 = (f32[16,16,64,128]{3,2,1,0:T(8,128)}, f32[8,16,16,256]{3,2,1,0:T(8,128)}) custom-call(f32[64]{0:T(128)} %kappa_ref.1, f32[1]{0:T(128)} %bitcast.tau_ref, f32[1]{0:T(128)} %bitcast.1.dt_ref, f32[16,16,256]{2,1,0:T(8,128)} %rho_ref.1, f32[3,16,16,256]{3,2,1,0:T(8,128)} %vel_ref.1, f32[3,16,16,256]{3,2,1,0:T(8,128)} %mag_ref.1, ...), custom_call_target="tpu_custom_call" | custom-call | flops 167772160 | bytes 16777216 | tf_op jit(solution)/shard_map/cosmic_ray/pallas_call | solution.py:800
  75.4 8.1 %deliver.1 = (f32[16,16,64,128]{3,2,1,0:T(8,128)}, f32[8,16,16,256]{3,2,1,0:T(8,128)}) custom-call(f32[16,16,64,128]{3,2,1,0:T(8,128)} %get-tuple-element.6.ray_in, f32[8,16,16,256]{3,2,1,0:T(8,128)} %get-tuple-element.7.fluid_in), custom_call_target="tpu_custom_call" | custom-call | tf_op jit(solution)/shard_map/deliver/pallas_call | solution.py:848

commit v2 on v1

--- a/solution.py
+++ b/solution.py
@@ -68,16 +68,18 @@
     state = [rho] + mom + list(b) + [energy]
     push = [mom[k] * v_n - b[k] * b_n for k in range(3)]
     push[normal] = push[normal] + total_p
-    turn = [v_n * b[k] - b_n * v[k] for k in range(3)]
+    turn = [None if k == normal else v_n * b[k] - b_n * v[k] for k in range(3)]
     work = (energy + total_p) * v_n - b_n * (v[0] * b[0] + v[1] * b[1] + v[2] * b[2])
-    speed = jnp.abs(v_n) + jnp.sqrt((ADIABATIC * pres + b_sq) / rho)
+    stiff = ADIABATIC * pres + b_sq
+    speed = jnp.abs(v_n) + stiff * lax.rsqrt(stiff * rho)
     return state, [mom[normal]] + push + turn + [work], speed
 
 
 def face_flux(low, high):
     wave = jnp.maximum(low[2], high[2])
+    jump = [wave * (high[0][n] - low[0][n]) for n in range(8)]
     return [
-        0.5 * ((low[1][n] + high[1][n]) - wave * (high[0][n] - low[0][n])) for n in range(8)
+        -jump[n] if low[1][n] is None else (low[1][n] + high[1][n]) - jump[n] for n in range(8)
     ]
 
 
@@ -529,7 +531,7 @@
     def fluid_step():
         radial = vel_ref.shape[3]
         spot = lax.broadcasted_iota(jnp.int32, (8, radial), 1)
-        scale = dt_ref[0] * inv_r_ref[0:8, :]
+        scale = 0.5 * dt_ref[0] * inv_r_ref[0:8, :]
 
         for start in range(0, rows, 8):
             here_rows = pl.ds(pl.multiple_of(band * rows + start, 8), 8)
@@ -556,11 +558,16 @@
 
                 outer = face_flux(
                     (state, flux, speed),
-                    ([ahead(x) for x in state], [ahead(x) for x in flux], ahead(speed)),
+                    (
+                        [ahead(x) for x in state],
+                        [None if x is None else ahead(x) for x in flux],
+                        ahead(speed),
+                    ),
                 )
                 scale_r = (1.0 / step_r) * scale
                 for n in range(8):
-                    inner = jnp.where(spot == 0, flux[n], pltpu.roll(outer[n], 1, 1))
+                    rim = 0.0 if flux[n] is None else 2.0 * flux[n]
+                    inner = jnp.where(spot == 0, rim, pltpu.roll(outer[n], 1, 1))
                     fluid[n, p, pl.ds(start, 8)] = state[n] - (
                         total[n] + scale_r * (outer[n] - inner)
                     )
@@ -634,14 +641,14 @@
             lax.fori_loop(0, azim, part, 0)
 
         def one(i, _):
-            for p in (2 * i, 2 * i + 1):
+            for p in [4 * i + j for j in range(4)]:
                 for part in range(rows // 8):
                     keep(
                         cells, p, apply(firsts, p, start + 8 * part, finish_second, 1, bins - 1)
                     )
             return 0
 
-        lax.fori_loop(0, azim // 2, one, 0)
+        lax.fori_loop(0, azim // 4, one, 0)
 
     def visit(i, _):
         s = (i + 1) // 2
@@ -674,12 +681,12 @@
             start = pl.multiple_of(block * rows, rows)
 
             def one(i, _):
-                for p in (2 * i, 2 * i + 1):
+                for p in [4 * i + j for j in range(4)]:
                     for part in range(rows // 8):
                         keep(firsts, p, apply(cells, p, start + 8 * part, finish_first, 0, bins))
                 return 0
 
-            lax.fori_loop(0, azim // 2, one, 0)
+            lax.fori_loop(0, azim // 4, one, 0)
             stage_out(1, firsts, start, rows)
             for way in range(2):
 

time: 83.7 us -> 82.6 us (0.987)
  Pallas kernels: 81.6 us -> 80.5 us
    pallas_call x1, Pallas kernels: 73.5 us -> 72.4 us  [cosmic_ray_step(): pl.pallas_call(functools.partial(cosmic_ray_kernel, bands, phis, spacing)...]
where the time goes in v2:
time: 82.6 us; the launch traced here: 82.5 us
  Pallas kernels  80.5 us (97%)
  between operations  1.93 us (2%)
    pallas_call x1, Pallas kernels, cosmic_ray_step(): pl.pallas_call(functools.partial(cosmic_ray_kernel, bands, phis, spacing)...  72.4 us
    pallas_call x1, Pallas kernels, cosmic_ray_step(): pl.pallas_call(deliver_kernel, out_shape=(jax.ShapeDtypeStruct(stepped.sh...  8.1 us

profile of v2, /device:TPU:0, one launch (start us, length us, event | category | flops | bytes accessed | tf_op | source)
XLA Modules:
  0.0 82.5 jit_solution(17517048121605311932)
XLA Ops:
  1.9 72.4 %cosmic_ray.1 = (f32[16,16,64,128]{3,2,1,0:T(8,128)}, f32[8,16,16,256]{3,2,1,0:T(8,128)}) custom-call(f32[64]{0:T(128)} %kappa_ref.1, f32[1]{0:T(128)} %bitcast.tau_ref, f32[1]{0:T(128)} %bitcast.1.dt_ref, f32[16,16,256]{2,1,0:T(8,128)} %rho_ref.1, f32[3,16,16,256]{3,2,1,0:T(8,128)} %vel_ref.1, f32[3,16,16,256]{3,2,1,0:T(8,128)} %mag_ref.1, ...), custom_call_target="tpu_custom_call" | custom-call | flops 167772160 | bytes 16777216 | tf_op jit(solution)/shard_map/cosmic_ray/pallas_call | solution.py:807
  74.4 8.1 %deliver.1 = (f32[16,16,64,128]{3,2,1,0:T(8,128)}, f32[8,16,16,256]{3,2,1,0:T(8,128)}) custom-call(f32[16,16,64,128]{3,2,1,0:T(8,128)} %get-tuple-element.6.ray_in, f32[8,16,16,256]{3,2,1,0:T(8,128)} %get-tuple-element.7.fluid_in), custom_call_target="tpu_custom_call" | custom-call | tf_op jit(solution)/shard_map/deliver/pallas_call | solution.py:855
